TPU v7x, 128 devices: a whole 4x4x4 slice. The times are simulated.
128 devices in a mesh: samp: 8 (over x, core), par: 16 (over y, z).
Axes of the slice: x: 4, y: 4, z: 4, core: 2. Of those that a mesh axis runs over, the one named last changes fastest.
Arguments:
- stream: float32 [512, 25, 512], P('samp'), may hold values from -48 to 48
- weight_in: bfloat16 [512, 2048], P('samp', 'par'), may hold values from -0.25 to 0.25
- weight_out: bfloat16 [2048, 512], P('par'), may hold values from -0.125 to 0.125
- readout: float32 [512], replicated, may hold values from -5 to 5
- spins: int32 [512, 100], replicated, may hold values from 0 to 1
- offdiag: float32 [512], replicated, may hold values from -18 to 18
Outputs:
- update: float32 [512, 2048], P('samp', 'par')
Inputs may be any that keep to these rules, and one draw needn't show every extreme that they name: `spins`: 1 marks an up spin, 0 a down spin.
All inputs are finite; a program needn't handle non-finite values.
Results may differ from a plain program's by a relative error of at most 0.02.
The roundings to bfloat16 on the way count: a program that leaves them out, or rounds other values in their place, can miss the bound.
Values may be sent and summed in bfloat16 or wider, within the bound.
A program may use at most 384 MiB of HBM per device.

v0:
```python
import math

import jax
import jax.numpy as jnp
from jax import lax
from jax.sharding import PartitionSpec as P

D = 512
FF = 2048


EPSILON = 1e-05
SHIFT_RATIO = 0.1
SECOND_RATIO = 0.5


def norm_rows(values):
    row_mean = jnp.mean(values, axis=-1, keepdims=True)
    centered = values - row_mean
    variance = jnp.mean(centered * centered, axis=-1, keepdims=True)
    return centered * lax.rsqrt(variance + EPSILON)


def gelu_back(preact, cotangent):
    _, backward = jax.vjp(jax.nn.gelu, preact)
    return backward(cotangent)[0]


def local_energy(spins, offdiag):
    side_sites = int(round_free_side(spins.shape[1]))
    spin_signs = (2 * spins - 1).astype(jnp.float32).reshape(spins.shape[0], side_sites, side_sites)
    right_spin = jnp.roll(spin_signs, -1, axis=2)
    down_spin = jnp.roll(spin_signs, -1, axis=1)
    diag_one = jnp.roll(down_spin, -1, axis=2)
    diag_two = jnp.roll(down_spin, 1, axis=2)
    near_bonds = jnp.sum(spin_signs * right_spin + spin_signs * down_spin, axis=(1, 2))
    far_bonds = jnp.sum(spin_signs * diag_one + spin_signs * diag_two, axis=(1, 2))
    return 0.25 * (near_bonds + SECOND_RATIO * far_bonds) + offdiag


def round_free_side(site_count):
    return math.isqrt(site_count)


def per_device(stream, weight_in, weight_out, readout, spins, offdiag):
    sample_rows, tokens, model_width = stream.shape
    samples = spins.shape[0]
    norm_scale = 1.0 / math.sqrt(samples)
    hidden = norm_rows(stream).astype(jnp.bfloat16)
    flat_rows = hidden.reshape(sample_rows * tokens, model_width)
    hidden_cols = weight_in.shape[1]
    preact = jnp.dot(
        flat_rows,
        lax.all_gather(weight_in, "samp", axis=0, tiled=True),
        preferred_element_type=jnp.float32,
    )
    activated = jax.nn.gelu(preact).astype(jnp.bfloat16)
    summed = lax.psum(jnp.dot(activated, weight_out, preferred_element_type=jnp.float32), "par")
    signal = (readout * jnp.tanh(summed)).astype(jnp.bfloat16)
    backward = lax.dot_general(
        signal, weight_out, (((1,), (1,)), ((), ())), preferred_element_type=jnp.float32
    )
    delta_rows = (
        gelu_back(preact, backward).astype(jnp.bfloat16).reshape(sample_rows, tokens, hidden_cols)
    )
    gradients = jnp.einsum(
        "std,stf->sdf", hidden, delta_rows, preferred_element_type=jnp.float32
    ).astype(jnp.bfloat16)
    gradient_panel = lax.all_to_all(gradients, "samp", split_axis=1, concat_axis=0, tiled=True)
    widened = gradient_panel.astype(jnp.float32)
    sample_mean = jnp.mean(widened, axis=0, keepdims=True)
    centered = ((widened - sample_mean) * norm_scale).astype(jnp.bfloat16).reshape(samples, -1)
    gram = lax.dot_general(
        centered, centered, (((1,), (1,)), ((), ())), preferred_element_type=jnp.float32
    )
    diag_shift = SHIFT_RATIO * jnp.trace(gram) / samples
    shifted = gram + diag_shift * jnp.eye(samples, dtype=jnp.float32)
    system = lax.psum(shifted, ("samp", "par"))
    lower_factor = jnp.linalg.cholesky(system)
    energies = local_energy(spins, offdiag)
    target = ((energies - jnp.mean(energies)) * norm_scale)[:, None]
    forward_solved = lax.linalg.triangular_solve(lower_factor, target, left_side=True, lower=True)
    solution = lax.linalg.triangular_solve(
        lower_factor, forward_solved, left_side=True, lower=True, transpose_a=True
    )
    coeffs = solution[:, 0].astype(jnp.bfloat16)
    result = jnp.dot(coeffs[None, :], centered, preferred_element_type=jnp.float32)
    return result.reshape(gradient_panel.shape[1], gradient_panel.shape[2]) * -math.sqrt(D * FF)


def solution(mesh):
    return jax.shard_map(
        per_device,
        mesh=mesh,
        in_specs=(P("samp", None, None), P("samp", "par"), P("par", None), P(), P(), P()),
        out_specs=P("samp", "par"),
        check_vma=False,
    )
```

profile of v0, /device:TPU:1, one launch (start us, length us, event | category | flops | bytes accessed | tf_op | source)
XLA Modules:
  0.0 615.9 jit_solution(10411298563935490412)
XLA Ops:
  6.5 2.4 reduce_sum.64
  8.9 2.5 multiply_reduce_fusion
  12.0 1.2 copy-done.3
  13.2 0.9 copy.37
  14.1 1.5 reshape.177
  15.6 14.9 %all_gather.3 = bf16[512,128]{1,0:T(8,128)(2,1)S(1)} all-gather(bf16[64,128]{1,0:T(8,128)(2,1)S(1)} %copy-done.6), channel_id=1, replica_groups=mesh['samp'=8,'par'=16] {'samp'}, dimensions={0}, use_global_device_ids=true | all-gather | bytes 147456 | tf_op jit(solution)/shard_map/all_gather | solution.py:54
  30.6 2.1 fusion.101
  32.7 2.3 fusion.36
  35.1 97.6 %all-reduce.4.cloned.1.call-done = f32[1600,512]{1,0:T(8,128)} async-done(((f32[1600,512]{1,0:T(8,128)}), f32[1600,512]{1,0:T(8,128)}) %all-reduce.4.cloned.1.call-update) | async-done | bytes 3276816 | tf_op jit(solution)/shard_map/psum | solution.py:58
  132.7 2.9 fusion.35
  135.7 5.7 convolution_convert_fusion
  141.4 12.0 %copy.38 = bf16[64,512,128]{2,0,1:T(8,128)(2,1)} copy(bf16[64,512,128]{2,1,0:T(8,128)(2,1)} %convolution_convert_fusion) | data formatting | bytes 16777216 | tf_op jit(solution)/shard_map/convert_element_type | solution.py:68
  153.4 6.0 all-to-all-start
  160.1 93.1 %all-to-all-done = bf16[64,512,128]{2,0,1:T(8,128)(2,1)} async-done(((bf16[64,512,128]{2,0,1:T(8,128)(2,1)}), bf16[64,512,128]{2,0,1:T(8,128)(2,1)}, u32[]{:S(2)}, u32[]{:S(2)}) %all-to-all-start) | async-done | bytes 8388640 | tf_op jit(solution)/shard_map/all_to_all | solution.py:69
  253.2 11.3 %bitcast_convert_fusion.3 = f32[64,8,64,128]{3,0,2,1:T(8,128)} fusion(bf16[64,512,128]{2,0,1:T(8,128)(2,1)} %all-to-all-done), kind=kLoop, calls=%fused_computation.173 | loop fusion | flops 4194304 | bytes 25165824 | tf_op jit(solution)/shard_map/convert_element_type | solution.py:70
  264.5 14.4 %bitcast_reduce_fusion = f32[64,128]{1,0:T(8,128)S(1)} fusion(f32[64,8,64,128]{3,0,2,1:T(8,128)} %bitcast_convert_fusion.3), kind=kLoop, calls=%fused_computation.6 | loop fusion | flops 4186112 | bytes 16809984 | tf_op jit(solution)/shard_map/reduce_sum | solution.py:71
  278.9 16.8 %fusion.3 = bf16[8,64,64,128]{3,2,1,0:T(8,128)(2,1)S(1)} fusion(f32[64,128]{1,0:T(8,128)S(1)} %get-tuple-element.48, f32[64,8,64,128]{3,0,2,1:T(8,128)} %bitcast_convert_fusion.3), kind=kLoop, calls=%fused_computation.8 | loop fusion | flops 12582912 | bytes 25198592 | tf_op jit(solution)/shard_map/convert_element_type | solution.py:72
  295.7 10.6 %select_reduce_fusion = (f32[]{:T(128)}, f32[512,512]{0,1:T(8,128)S(1)}) fusion(bf16[512,64,128]{2,1,0:T(8,128)(2,1)S(1)} %bitcast.195), kind=kOutput, calls=%fused_computation.54 | convolution fusion | flops 4295753728 | bytes 9437188 | tf_op jit(solution)/shard_map/dot_general | solution.py:73
  307.0 1.1 select_add_fusion
  308.2 0.7 fusion.97
  309.6 14.1 %copy.39 = f32[64,8,64,128]{3,2,0,1:T(8,128)} copy(bf16[64,8,64,128]{3,0,2,1:T(8,128)(2,1)} %bitcast.56) | data formatting | bytes 25165824 | tf_op jit(solution)/shard_map/convert_element_type | solution.py:70
  323.8 129.0 %all-reduce.6.cloned.1.call-done = f32[512,512]{0,1:T(8,128)} async-done(((f32[512,512]{0,1:T(8,128)}), f32[512,512]{0,1:T(8,128)}) %all-reduce.6.cloned.1.call-update) | async-done | bytes 1048592 | tf_op jit(solution)/shard_map/psum | solution.py:78
  452.7 1.6 copy.44
  454.3 1.4 fusion.28
  455.8 11.7 %cholesky.103 = f32[128,128]{1,0:T(8,128)S(1)} custom-call(f32[128,128]{1,0:T(8,128)S(1)} %cholesky.263), custom_call_target="Cholesky" | custom-call | tf_op jit(solution)/shard_map/jit(cholesky)/cholesky | solution.py:79
  467.5 9.8 %custom-call.32 = f32[1,128,128]{1,2,0:T(8,128)S(1)} custom-call(f32[1,128,128]{2,1,0:T(8,128)S(1)} %get-tuple-element.46), custom_call_target="InvertDiagBlocksLowerTriangular" | custom-call | tf_op jit(solution)/shard_map/jit(cholesky)/cholesky | solution.py:79
  478.0 11.9 %cholesky.215 = f32[128,128]{1,0:T(8,128)S(1)} custom-call(f32[128,128]{1,0:T(8,128)S(1)} %cholesky.267), custom_call_target="Cholesky" | custom-call | tf_op jit(solution)/shard_map/jit(cholesky)/cholesky | solution.py:79
  490.4 9.8 %custom-call.33 = f32[1,128,128]{1,2,0:T(8,128)S(1)} custom-call(f32[1,128,128]{2,1,0:T(8,128)S(1)} %get-tuple-element.44), custom_call_target="InvertDiagBlocksLowerTriangular" | custom-call | tf_op jit(solution)/shard_map/jit(cholesky)/cholesky | solution.py:79
  500.6 0.6 convolution_subtract_fusion.1
  501.2 11.7 %cholesky.236 = f32[128,128]{1,0:T(8,128)S(1)} custom-call(f32[128,128]{1,0:T(8,128)S(1)} %cholesky.272), custom_call_target="Cholesky" | custom-call | tf_op jit(solution)/shard_map/jit(cholesky)/cholesky | solution.py:79
  513.1 9.8 %custom-call.34 = f32[1,128,128]{1,2,0:T(8,128)S(1)} custom-call(f32[1,128,128]{2,1,0:T(8,128)S(1)} %get-tuple-element.42), custom_call_target="InvertDiagBlocksLowerTriangular" | custom-call | tf_op jit(solution)/shard_map/jit(cholesky)/cholesky | solution.py:79
  523.2 0.9 convolution_subtract_fusion.2
  524.1 11.7 %cholesky.253 = f32[128,128]{1,0:T(8,128)S(1)} custom-call(f32[128,128]{1,0:T(8,128)S(1)} %convolution_subtract_fusion.2), custom_call_target="Cholesky" | custom-call | tf_op jit(solution)/shard_map/jit(cholesky)/cholesky | solution.py:79
  535.9 0.6 compare_reduce_fusion.1
  536.6 0.7 compare_reduce_fusion
  537.3 0.7 compare_reduce_fusion.2
  540.6 8.6 %while.1 = (s32[]{:T(128)}, f32[512,512]{0,1:T(8,128)S(1)}, s32[4,2]{0,1:T(2,128)S(1)}, f32[4,128,128]{2,1,0:T(8,128)S(1)}, s32[]{:T(128)}) while((s32[]{:T(128)}, f32[512,512]{0,1:T(8,128)S(1)}, s32[4,2]{0,1:T(2,128)S(1)}, f32[4,128,128]{2,1,0:T(8,128)S(1)}, s32[]{:T(128)}) %tuple.34), condition=%wide.while_cond, body=%wide.while_body.sunk | while | flops 2 | bytes 393321 | solution.py:83
  540.7 0.6 fusion.119
  541.3 1.3 dynamic-slice.7
  542.8 0.6 fusion.119
  543.4 1.3 dynamic-slice.7
  545.0 0.6 fusion.119
  545.6 1.3 dynamic-slice.7
  547.1 0.6 fusion.119
  547.7 1.3 dynamic-slice.7
  549.2 39.3 %custom-call.35 = f32[4,128,128]{1,2,0:T(8,128)S(1)} custom-call(f32[4,128,128]{2,1,0:T(8,128)S(1)} %get-tuple-element.12), custom_call_target="InvertDiagBlocksLowerTriangular" | custom-call | tf_op jit(solution)/shard_map/triangular_solve | solution.py:83
  591.5 16.8 %fusion.5 = f32[1,64,128]{2,0,1:T(1,128)S(1)} fusion(bf16[512,1,1]{0,1,2:T(2,128)(2,1)S(1)} %reshape.237, f32[64,8,64,128]{3,2,1,0:T(8,128)} %bitcast.194, f32[8192]{0:T(1024)S(1)} %get-tuple-element.47), kind=kOutput, calls=%fused_computation.10 | convolution fusion | flops 20971520 | bytes 16843776 | tf_op jit(solution)/shard_map/dot_general | solution.py:87
  608.3 0.6 broadcast_multiply_fusion
  (93 shorter events, 7.4 us)
Async XLA Ops:
  6.5 26.2 %copy-start = (bf16[128,512]{1,0:T(8,128)(2,1)S(1)}, bf16[128,512]{1,0:T(8,128)(2,1)}, u32[]{:S(2)}) copy-start(bf16[128,512]{1,0:T(8,128)(2,1)} %param.8) | copy-start | bytes 393220
  6.5 4.9 copy-start.2
  6.5 126.1 %all-reduce.4.cloned.1.call-start = ((), (), s32[]{:S(2)}) async-start(), calls=%async_computation.1 | async-start | bytes 6553600 | tf_op jit(solution)/shard_map/psum | solution.py:58
  8.9 6.7 %copy-start.6 = (bf16[64,128]{1,0:T(8,128)(2,1)S(1)}, bf16[64,128]{1,0:T(8,128)(2,1)}, u32[]{:S(2)}) copy-start(bf16[64,128]{1,0:T(8,128)(2,1)} %param.7) | copy-start | bytes 49156
  12.0 1.2 copy-start.3
  13.2 119.5 %copy-start.8 = (f32[512]{0:T(512)S(1)}, f32[512]{0:T(512)}, u32[]{:S(2)}) copy-start(f32[512]{0:T(512)} %param.9) | copy-start | bytes 6148
  30.6 105.1 %copy-start.4 = (bf16[64,25,512]{2,0,1:T(8,128)(2,1)S(1)}, bf16[64,25,512]{2,0,1:T(8,128)(2,1)}, u32[]{:S(2)}) copy-start(bf16[64,25,512]{2,0,1:T(8,128)(2,1)} %copy-done.3) | copy-start | bytes 4915204
  153.4 6.2 copy-start.5
  153.4 99.8 %all-to-all-start = ((bf16[64,512,128]{2,0,1:T(8,128)(2,1)}), bf16[64,512,128]{2,0,1:T(8,128)(2,1)}, u32[]{:S(2)}, u32[]{:S(2)}) async-start(bf16[64,512,128]{2,0,1:T(8,128)(2,1)} %copy.38), calls=%async_computation | async-start | bytes 16777216 | tf_op jit(solution)/shard_map/all_to_all | solution.py:69
  159.3 293.4 %all-reduce.6.cloned.1.call-start = ((), (), s32[]{:S(2)}) async-start(), calls=%async_computation.2 | async-start | bytes 2097152 | tf_op jit(solution)/shard_map/psum | solution.py:78
  295.7 12.5 %copy-start.7 = (f32[512]{0:T(512)S(1)}, f32[512]{0:T(512)}, u32[]{:S(2)}) copy-start(f32[512]{0:T(512)} %param.11) | copy-start | bytes 6148
  591.5 17.4 %copy-start.1 = (bf16[128,512]{1,0:T(8,128)(2,1)S(1)}, bf16[128,512]{1,0:T(8,128)(2,1)}, u32[]{:S(2)}) copy-start(bf16[128,512]{1,0:T(8,128)(2,1)} %param.8) | copy-start | bytes 393220
Sparse Core Ops, SparseCore 0:
  35.2 97.4 all-reduce.3
  308.2 144.4 all-reduce.5
where the time goes:
time: 619 us; the launch traced here: 616 us
  waiting for transfers between devices  320 us (52%)
  other arithmetic  170 us (27%)
  matrix products  46 us (7%)
  local copies, waits for them, and re-layouts  40.7 us (7%)
  between operations  18 us (3%)
  blocking collectives  14.9 us (2%)
    psum x1, waiting for transfers between devices, per_device(): system = lax.psum(shifted, ('samp', 'par'))  129 us
    psum x1, waiting for transfers between devices, per_device(): lax.psum(jnp.dot(activated, weight_out, preferred_element_type=jnp.float3...  97.6 us
    all_to_all x1, waiting for transfers between devices, per_device(): lax.all_to_all(gradients, 'samp', split_axis=1, concat_axis=0, tiled=True)  93.1 us
    another operation x14, other arithmetic, per_device(): lower_factor = jnp.linalg.cholesky(system)  78.6 us
    another operation x4, other arithmetic, per_device(): lax.linalg.triangular_solve(lower_factor, forward_solved, left_side=True,...  39.5 us
    convert_element_type x1, other arithmetic, per_device(): ((widened - sample_mean) * norm_scale).astype(jnp.bfloat16)  16.8 us
    dot_general x1, matrix products, per_device(): jnp.dot(coeffs[None, :], centered, preferred_element_type=jnp.float32)  16.8 us
    all_gather x1, blocking collectives, per_device(): lax.all_gather(weight_in, 'samp', axis=0, tiled=True)  14.9 us
  transfers between devices with their start and end apart: 3, of which 3 were waited for; matrix products, arithmetic and copies ran while one was open for 2% of the time, Pallas kernels for 0%

commit v1 on v0

v1 whole, which is shorter than its diff:
```python
import functools
import math

import jax
import jax.numpy as jnp
from jax import lax
from jax.experimental import pallas as pl
from jax.experimental.pallas import tpu as pltpu
from jax.sharding import PartitionSpec as P

D = 512
FF = 2048
EPSILON = 1e-05
SHIFT_RATIO = 0.1
SECOND_RATIO = 0.5
MESH = pl.DeviceIdType.MESH
F32 = jnp.float32
BF16 = jnp.bfloat16
HI = lax.Precision.HIGHEST


def dot_nn(a, b):
    return lax.dot_general(a, b, (((1,), (0,)), ((), ())), precision=HI, preferred_element_type=F32)


def dot_nt(a, b):
    return lax.dot_general(a, b, (((1,), (1,)), ((), ())), precision=HI, preferred_element_type=F32)


def thirds(values):
    high = values.astype(BF16).astype(F32)
    rest = values - high
    middle = rest.astype(BF16).astype(F32)
    return high, middle, rest - middle


def outer(left, right):
    a, b, c = thirds(left)
    d, e, f = thirds(right)
    lhs = jnp.concatenate([a, a, b, a, b, c], axis=0).astype(BF16)
    rhs = jnp.concatenate([d, e, d, f, e, d], axis=0).astype(BF16)
    return lax.dot_general(lhs, rhs, (((0,), (0,)), ((), ())), preferred_element_type=F32)


def spread_column(values, at):
    return jnp.broadcast_to(values[:, at : at + 1], (8, 128))


def sweep_block(block):
    lane = lax.broadcasted_iota(jnp.int32, (8, 128), 1)
    sub = lax.broadcasted_iota(jnp.int32, (8, 128), 0)
    rows = [block[8 * r : 8 * r + 8, :] for r in range(16)]
    for g in range(16):
        panel = rows[g]
        before = panel
        splat = [spread_column(panel, 8 * g + m) for m in range(8)]
        for i in range(8):
            unit = jnp.where(sub == i, 1.0, 0.0)
            pivot = jnp.broadcast_to(splat[i][i : i + 1, :], (8, 128))
            factor = (splat[i] - unit) * (1.0 / pivot)
            panel = jnp.where(lane == 8 * g + i, unit, panel)
            panel = panel - factor * jnp.broadcast_to(panel[i : i + 1, :], (8, 128))
            for m in range(i + 1, 8):
                splat[m] = splat[m] - factor * jnp.broadcast_to(splat[m][i : i + 1, :], (8, 128))
        inside = (lane >= 8 * g) & (lane < 8 * g + 8)
        panel = jnp.where(inside, -panel, panel)
        change = outer(before, panel)
        for r in range(16):
            if r == g:
                continue
            kept = jnp.where(inside, 0.0, rows[r])
            if r == g + 1:
                for m in range(8):
                    kept = kept - spread_column(rows[r], 8 * g + m) * jnp.broadcast_to(panel[m : m + 1, :], (8, 128))
                rows[r] = kept
            else:
                rows[r] = kept - change[8 * r : 8 * r + 8, :]
        rows[g] = panel
    return jnp.concatenate(rows, axis=0)


def solve_kernel(shift_ratio, scale, samples, gram_ref, target_ref, cent_hbm, out_ref, a_ref, w_ref, cent, sems):
    blocks = samples // 128
    chunks = sems.shape[0]
    wide = cent.shape[1] // chunks

    def load(m):
        at = pl.ds(m * wide, wide)
        return pltpu.make_async_copy(cent_hbm.at[:, at], cent.at[:, at], sems.at[m])

    for m in range(chunks):
        load(m).start()
    eye = lax.broadcasted_iota(jnp.int32, (128, 128), 0) == lax.broadcasted_iota(jnp.int32, (128, 128), 1)
    base = [0]
    for k in range(blocks):
        base.append(base[-1] + samples - 128 * k)
    trace = jnp.zeros((1, 1), F32)
    for k in range(blocks):
        trace += jnp.sum(jnp.where(eye, gram_ref[base[k] : base[k] + 128, :], 0.0), axis=(0, 1), keepdims=True)
    shift = shift_ratio * trace / samples
    shift = jnp.where(eye, jnp.broadcast_to(shift, (128, 128)), 0.0)
    rhs = []
    for k in range(blocks):
        a_ref[base[k] : base[k] + 128, :] = gram_ref[base[k] : base[k] + 128, :] + shift
        if k < blocks - 1:
            a_ref[base[k] + 128 : base[k + 1], :] = gram_ref[base[k] + 128 : base[k + 1], :]
        rhs.append(jnp.broadcast_to(target_ref[0:1, 128 * k : 128 * k + 128], (8, 128)))
    for k in range(blocks):
        inv = -sweep_block(a_ref[base[k] : base[k] + 128, :])
        if k < blocks - 1:
            below = a_ref[base[k] + 128 : base[k + 1], :]
            w = dot_nn(below, inv)
            w_ref[base[k] + 128 : base[k + 1], :] = w
            drop = dot_nt(rhs[k], w)
            for j in range(k + 1, blocks):
                at = 128 * (j - k - 1)
                a_ref[base[j] : base[j + 1], :] -= dot_nt(w[at:], below[at : at + 128])
                rhs[j] = rhs[j] - drop[:, at : at + 128]
        rhs[k] = dot_nn(rhs[k], inv)
    found = [None] * blocks
    for k in reversed(range(blocks)):
        x = rhs[k]
        for i in range(k + 1, blocks):
            r = base[k] + 128 * (i - k)
            x = x - dot_nn(found[i], w_ref[r : r + 128, :])
        found[k] = x
    coeffs = jnp.concatenate(found, axis=1).astype(BF16)
    for m in range(chunks):
        load(m).wait()
        part = jnp.dot(coeffs, cent[:, m * wide : (m + 1) * wide], preferred_element_type=F32) * scale
        for i in range(wide // 128):
            r = m * wide // 128 + i
            out_ref[r : r + 1, :] = part[0:1, 128 * i : 128 * (i + 1)]


def solve(gram, target, centered):
    samples, width = centered.shape
    blocks = samples // 128
    rows = blocks * (blocks + 1) // 2 * 128
    vmem = pl.BlockSpec(memory_space=pltpu.VMEM)
    return pl.pallas_call(
        functools.partial(solve_kernel, SHIFT_RATIO, -math.sqrt(D * FF), samples),
        out_shape=jax.ShapeDtypeStruct((width // 128, 128), F32),
        in_specs=[vmem, vmem, pl.BlockSpec(memory_space=pl.ANY)],
        out_specs=vmem,
        scratch_shapes=[
            pltpu.VMEM((rows, 128), F32),
            pltpu.VMEM((rows, 128), F32),
            pltpu.VMEM((samples, width), BF16),
            pltpu.SemaphoreType.DMA((8,)),
        ],
        compiler_params=pltpu.CompilerParams(vmem_limit_bytes=60 << 20),
        name="solve",
    )(gram, target, centered)


GROUP = 4
WIDE = 8 * 65


def enter(ids):
    barrier = pltpu.get_barrier_semaphore()
    for device in ids:
        pl.semaphore_signal(barrier, inc=1, device_id=device, device_id_type=MESH)
    pl.semaphore_wait(barrier, len(ids))


def remote(src, dst, send, recv, device):
    copy = pltpu.make_async_remote_copy(
        src_ref=src, dst_ref=dst, send_sem=send, recv_sem=recv, device_id=device, device_id_type=MESH
    )
    copy.start()
    return copy


def describe(src, dst, send, recv, device):
    return pltpu.make_async_remote_copy(
        src_ref=src, dst_ref=dst, send_sem=send, recv_sem=recv, device_id=device, device_id_type=MESH
    )


def each(first, last, body):
    def step(k, carry):
        body(k)
        return carry

    lax.fori_loop(first, last, step, 0)


def forward_kernel(
    stream_ref, win_ref, wout_ref, readout_ref, hall_ref, dl_ref,
    win, wout, hid, ht, slope, acc, dsend,
    xs, xr, ws, wr, vs, vr, wws, wwr, vvs, vvr, sws, swr, svs, svr, hs, hr, ls, lr, own,
):
    s, p = lax.axis_index("samp"), lax.axis_index("par")
    x, c = s // 2, lax.rem(s, 2)
    y, z = p // 4, lax.rem(p, 4)
    sibling = s + 1 - 2 * c
    n = 16
    groups, tokens = 16, 25
    rows = hid.shape[0]
    enter([(s, lax.rem(p + k, n)) for k in range(1, n)] + [(lax.rem(s + k, 8), p) for k in range(1, 8)])

    def at(a, b):
        return lax.rem(y + a, 4) * 4 + lax.rem(z + b, 4)

    def origin(a, b):
        return at(4 - a, 4 - b)

    def xcopy(k):
        return describe(win_ref, win.at[p, x, c], xs.at[k - 1], xr.at[k - 1], (lax.rem(s + 2 * k, 8), p))

    def w_first(k):
        return describe(win.at[p, :, c], win.at[p, :, c], ws.at[k - 1], wr.at[k - 1], (s, at(k, 0)))

    def w_then(a, m):
        q, i = origin(a, 0), 3 * a + m - 1
        return describe(win.at[q, :, c], win.at[q, :, c], wws.at[i], wwr.at[i], (s, at(0, m)))

    def v_first(k):
        return describe(wout.at[p, c], wout.at[p, c], vs.at[k - 1], vr.at[k - 1], (s, at(0, k)))

    def v_then(b, m):
        q, i = origin(0, b), 3 * b + m - 1
        return describe(wout.at[q, c], wout.at[q, c], vvs.at[i], vvr.at[i], (s, at(m, 0)))

    def w_across(i):
        q = origin(i // 4, lax.rem(i, 4))
        return describe(win.at[q, :, c], win.at[q, :, c], sws.at[i], swr.at[i], (sibling, p))

    def v_across(i):
        q = origin(i // 4, lax.rem(i, 4))
        return describe(wout.at[q, c], wout.at[q, c], svs.at[i], svr.at[i], (sibling, p))

    def hcopy(k):
        to = lax.rem(s + k, 8)
        return describe(ht.at[to], hall_ref.at[s], hs.at[k - 1], hr.at[k - 1], (to, p))

    def lcopy(k):
        q = lax.rem(p + k, n)
        return describe(dsend.at[q], dl_ref.at[p], ls.at[k - 1], lr.at[k - 1], (s, q))

    mine_w = pltpu.make_async_copy(win_ref, win.at[p, x, c], own.at[0])
    mine_v = pltpu.make_async_copy(wout_ref.at[pl.ds(pl.multiple_of(64 * c, 64), 64)], wout.at[p, c], own.at[1])
    mine_w.start()
    mine_v.start()
    each(1, 4, lambda k: xcopy(k).start())
    mine_v.wait()
    each(1, 4, lambda k: v_first(k).start())
    each(1, 4, lambda m: v_then(0, m).start())
    v_across(0).start()
    mine_w.wait()

    def prepare(pair):
        values = stream_ref[:, pl.ds(pl.multiple_of(8 * pair, 8), 8), :]
        mean = jnp.mean(values, axis=-1, keepdims=True)
        centered = values - mean
        variance = jnp.mean(centered * centered, axis=-1, keepdims=True)
        scaled = centered * lax.rsqrt(variance + EPSILON)
        for half in range(2):
            g = 2 * pair + half
            hidden = jnp.concatenate(
                [scaled[t, 4 * half : 4 * half + 4] for t in range(tokens)] + [jnp.zeros((128 - 4 * tokens, 512), F32)], axis=0
            )

            @pl.when(g == p)
            def _():
                hid[...] = hidden[:rows].astype(BF16)

            flipped = jnp.transpose(hidden).astype(BF16)
            for q in range(8):
                ht[q, g] = flipped[64 * q : 64 * (q + 1), :]

    def open_w():
        each(1, 4, lambda k: xcopy(k).wait_recv())
        each(1, 4, lambda k: w_first(k).start())
        each(1, 4, lambda m: w_then(0, m).start())
        w_across(0).start()

    def pass_v(k):
        v_first(k).wait_recv()
        each(1, 4, lambda m: v_then(k, m).start())
        v_across(k).start()

    def pass_w(k):
        w_first(k).wait_recv()
        each(1, 4, lambda m: w_then(k, m).start())
        w_across(4 * k).start()

    def work(step):
        prepare(step)

        @pl.when(step == 0)
        def _():
            open_w()

        @pl.when(step == 2)
        def _():
            each(1, 4, pass_v)

        @pl.when(step == 4)
        def _():
            each(1, 4, pass_w)

    each(0, groups // 2, work)
    each(1, 8, lambda k: hcopy(k).start())
    mine_h = pltpu.make_async_copy(ht.at[s], hall_ref.at[s], own.at[2])
    mine_h.start()
    acc[...] = jnp.zeros_like(acc)

    def take(i):
        a, b = i // 4, lax.rem(i, 4)

        @pl.when(b > 0)
        def _():
            w_then(a, b).wait_recv()
            w_across(i).start()

        @pl.when(a > 0)
        def _():
            v_then(b, a).wait_recv()
            v_across(i).start()

    def compute(i):
        q = origin(i // 4, lax.rem(i, 4))
        w_across(i).wait_recv()
        v_across(i).wait_recv()
        preact = jnp.dot(hid[...], win[q].reshape(512, 128), preferred_element_type=F32)
        active, pull = jax.vjp(jax.nn.gelu, preact)
        slope[q] = pull(jnp.ones_like(preact))[0]
        acc[...] += jnp.dot(active.astype(BF16), wout[q].reshape(128, 512), preferred_element_type=F32)

    take(0)

    def both(i):
        take(i)
        compute(i - 1)

    each(1, n, both)
    compute(n - 1)
    signal = (readout_ref[...] * jnp.tanh(acc[...])).astype(BF16)

    def back(k):
        j = lax.rem(p // 2 + k, 8)
        weights = wout[pl.ds(2 * j, 2)].reshape(256, 512)
        backward = lax.dot_general(signal, weights, (((1,), (1,)), ((), ())), preferred_element_type=F32)
        for u in range(2):
            q = 2 * j + u
            dsend[q] = (backward[:, 128 * u : 128 * (u + 1)] * slope[q]).astype(BF16)

            @pl.when(q != p)
            def _():
                lcopy(lax.rem(q - p + n, n)).start()

    each(1, 9, back)
    dl_ref[p] = dsend[p]
    each(1, n, lambda k: lcopy(k).wait())
    each(1, 8, lambda k: hcopy(k).wait())
    mine_h.wait()
    each(1, 4, lambda k: xcopy(k).wait_send())
    each(1, 4, lambda k: w_first(k).wait_send())
    each(1, 4, lambda k: v_first(k).wait_send())
    each(0, 4, lambda k: each(1, 4, lambda m: w_then(k, m).wait_send()))
    each(0, 4, lambda k: each(1, 4, lambda m: v_then(k, m).wait_send()))
    each(0, n, lambda i: w_across(i).wait_send())
    each(0, n, lambda i: v_across(i).wait_send())


def forward(stream, weight_in, weight_out, readout):
    rows = 112
    sem = pltpu.SemaphoreType.DMA
    vmem = pl.BlockSpec(memory_space=pltpu.VMEM)
    return pl.pallas_call(
        forward_kernel,
        out_shape=[jax.ShapeDtypeStruct((8, 16, 64, 128), BF16), jax.ShapeDtypeStruct((16, rows, 128), BF16)],
        in_specs=[vmem] * 4,
        out_specs=[pl.BlockSpec(memory_space=pl.ANY), vmem],
        scratch_shapes=[
            pltpu.VMEM((16, 4, 2, 64, 128), BF16),
            pltpu.VMEM((16, 2, 64, 512), BF16),
            pltpu.VMEM((rows, 512), BF16),
            pltpu.VMEM((8, 16, 64, 128), BF16),
            pltpu.VMEM((16, rows, 128), F32),
            pltpu.VMEM((rows, 512), F32),
            pltpu.VMEM((16, rows, 128), BF16),
        ]
        + [sem((3,))] * 6
        + [sem((12,))] * 4
        + [sem((16,))] * 4
        + [sem((7,))] * 2
        + [sem((15,))] * 2
        + [sem((3,))],
        compiler_params=pltpu.CompilerParams(collective_id=3, has_side_effects=True, vmem_limit_bytes=56 << 20),
        name="forward",
    )(stream, weight_in, weight_out, readout)


def gather_gram_kernel(
    hall_ref, dl_ref, cent_out, gram_ref, ht, dall, grad, cent, part_ref, twin, first, second,
    sr, rr, sl, rl, fr, qr, fl, ql, bs, br, s0, r0, s1, r1, s2, r2, s3, r3, s4, r4, own, outs,
):
    s, p = lax.axis_index("samp"), lax.axis_index("par")
    sibling = s + 1 - 2 * lax.rem(s, 2)
    right, left, far = lax.rem(s + 2, 8), lax.rem(s + 6, 8), lax.rem(s + 4, 8)
    pars = [lax.rem(p + k, 16) for k in range(1, 16)]
    samps = [lax.rem(s + k, 8) for k in range(1, 8)]
    dims, width, rows, tokens, samples = 64, 128, 112, 25, 512
    norm_scale = 1.0 / math.sqrt(samples)
    mine_h = pltpu.make_async_copy(hall_ref, ht, own.at[0])
    mine_d = pltpu.make_async_copy(dl_ref, dall.at[s], own.at[1])
    mine_h.start()
    mine_d.start()
    enter([(s, q) for q in pars] + [(q, p) for q in samps])

    def part(origin, c):
        return dall.at[origin, pl.ds(pl.multiple_of(4 * c, 4), 4)]

    def to_right(c):
        return describe(part(s, c), part(s, c), sr.at[c], rr.at[c], (right, p))

    def to_left(c):
        return describe(part(s, c), part(s, c), sl.at[c], rl.at[c], (left, p))

    def on_right(c):
        return describe(part(left, c), part(left, c), fr.at[c], qr.at[c], (right, p))

    def on_left(c):
        return describe(part(right, c + 2), part(right, c + 2), fl.at[c], ql.at[c], (left, p))

    def across(origin, c, slot):
        return describe(part(origin, c), part(origin, c), bs.at[slot], br.at[slot], (sibling, p))

    mine_d.wait()

    def begin(c):
        to_right(c).start()
        to_left(lax.rem(c + 2, 4)).start()

    each(0, 4, begin)
    each(0, 4, lambda c: across(s, c, c).start())
    mine_h.wait()

    lane = lax.broadcasted_iota(jnp.int32, (dims, width), 1)
    keep = [(lax.rem(lane, GROUP) == i) & (lane < tokens * GROUP) for i in range(GROUP)]
    fill = jnp.zeros((width - rows, 128), BF16)
    nothing = jnp.zeros((dims, width), BF16)

    def make(origin, c):
        for u in range(4):
            group = 4 * c + u
            flipped = ht[origin, group]
            delta = jnp.concatenate([dall[origin, group], fill], axis=0)
            stack = jnp.concatenate([jnp.where(keep[i], flipped, nothing) for i in range(GROUP)], axis=0)
            grads = jnp.dot(stack, delta, preferred_element_type=F32).astype(BF16).astype(F32)
            for i in range(GROUP):
                grad[pl.ds(64 * origin + GROUP * group + i, dims, stride=WIDE), :] = grads[dims * i : dims * (i + 1), :]

    each(0, 4, lambda c: make(s, c))

    def near(c):
        d = lax.rem(c + 2, 4)
        to_right(c).wait_recv()

        @pl.when(c < 2)
        def _():
            on_right(c).start()

        across(left, c, 4 + c).start()
        to_left(d).wait_recv()

        @pl.when(c < 2)
        def _():
            on_left(c).start()

        across(right, d, 8 + d).start()
        make(left, c)
        make(right, d)

    each(0, 4, near)

    def beside(c):
        across(s, c, c).wait_recv()
        make(sibling, c)

    each(0, 4, beside)

    def opposite(c):
        on_right(c).wait_recv()
        across(far, c, 12 + c).start()
        on_left(c).wait_recv()
        across(far, c + 2, 14 + c).start()
        make(far, c)
        make(far, c + 2)

    each(0, 2, opposite)

    def near_beside(c):
        across(left, c, 4 + c).wait_recv()
        across(right, c, 8 + c).wait_recv()
        make(sibling + left - s, c)
        make(sibling + right - s, c)

    each(0, 4, near_beside)

    def far_beside(c):
        across(far, c, 12 + c).wait_recv()
        across(far, c + 2, 14 + c).wait_recv()
        make(sibling + far - s, c)
        make(sibling + far - s, c + 2)

    each(0, 2, far_beside)

    count = 4

    def center(m):
        for half in range(count):
            d = count * m + half
            values = grad[d * WIDE : d * WIDE + samples, :]
            mean = jnp.sum(values, axis=0, keepdims=True) * (1.0 / samples)
            cent[:, d * 128 : (d + 1) * 128] = ((values - mean) * norm_scale).astype(BF16)

    def store(m):
        at = pl.ds(m * 128 * count, 128 * count)
        return pltpu.make_async_copy(cent.at[:, at], cent_out.at[:, at], outs.at[m])

    def add(m):
        block = cent[:, m * 128 * count : (m + 1) * 128 * count]
        low = lax.dot_general(block, block[:256], (((1,), (1,)), ((), ())), preferred_element_type=F32)
        high = lax.dot_general(block[256:], block[256:], (((1,), (1,)), ((), ())), preferred_element_type=F32)
        for a, b, term in [(0, 512, low[:, :128]), (512, 896, low[128:, 128:]), (896, 1152, high[:, :128]), (1152, 1280, high[128:, 128:])]:
            if m == 0:
                part_ref[a:b, :] = term
            else:
                part_ref[a:b, :] += term

    steps = dims // count
    center(0)
    store(0).start()
    for m in range(1, steps):
        center(m)
        store(m).start()
        add(m - 1)
    add(steps - 1)

    core = lax.rem(s, 2)
    x = s // 2

    def slot(half, q):
        return pl.ds(pl.multiple_of(640 * half + 40 * q, 8), 40)

    give = pl.ds(pl.multiple_of(640 * (1 - core), 640), 640)
    keeps = pl.ds(pl.multiple_of(640 * core, 640), 640)
    copy = remote(part_ref.at[give], twin, s0.at[0], r0.at[0], (sibling, p))
    copy.wait_recv()
    part_ref[keeps, :] += twin[...]
    copies = [remote(part_ref.at[slot(core, q)], first.at[p], s1.at[k], r1.at[k], (s, q)) for k, q in enumerate(pars)]
    first[p] = part_ref[slot(core, p), :]
    for each_copy in copies:
        each_copy.wait_recv()
    total = first[0]
    for q in range(1, 16):
        total = total + first[q]
    second[x] = total
    more = [remote(second.at[x], second.at[x], s2.at[k], r2.at[k], (q, p)) for k, q in enumerate([right, far, left])]
    for each_copy in more:
        each_copy.wait_recv()
    total = second[0]
    for q in range(1, 4):
        total = total + second[q]
    gram_ref[slot(core, p), :] = total
    here = gram_ref.at[slot(core, p)]
    spread = [remote(here, here, s3.at[k], r3.at[k], (s, q)) for k, q in enumerate(pars)]
    passed = [remote(here, here, s4.at[15], r4.at[15], (sibling, p))]
    for k in range(15):
        spread[k].wait_recv()
        there = gram_ref.at[slot(core, lax.rem(p + 15 - k, 16))]
        passed.append(remote(there, there, s4.at[k], r4.at[k], (sibling, p)))
    for each_copy in passed:
        each_copy.wait()
    copy.wait_send()
    for each_copy in copies + more + spread:
        each_copy.wait_send()
    each(0, 4, lambda c: to_right(c).wait_send())
    each(0, 4, lambda c: to_left(c).wait_send())
    each(0, 2, lambda c: on_right(c).wait_send())
    each(0, 2, lambda c: on_left(c).wait_send())
    each(0, 16, lambda c: across(s, 0, c).wait_send())
    for m in range(steps):
        store(m).wait()


def gather_gram(ht_all, delta):
    sem = pltpu.SemaphoreType.DMA
    return pl.pallas_call(
        gather_gram_kernel,
        out_shape=[jax.ShapeDtypeStruct((512, 8192), BF16), jax.ShapeDtypeStruct((1280, 128), F32)],
        in_specs=[pl.BlockSpec(memory_space=pl.ANY)] * 2,
        out_specs=[pl.BlockSpec(memory_space=pl.ANY), pl.BlockSpec(memory_space=pltpu.VMEM)],
        scratch_shapes=[
            pltpu.VMEM((8, 16, 64, 128), BF16),
            pltpu.VMEM((8, 16, 112, 128), BF16),
            pltpu.VMEM((64 * WIDE, 128), F32),
            pltpu.VMEM((512, 8192), BF16),
            pltpu.VMEM((1280, 128), F32),
            pltpu.VMEM((640, 128), F32),
            pltpu.VMEM((16, 40, 128), F32),
            pltpu.VMEM((4, 40, 128), F32),
        ]
        + [sem((4,))] * 4
        + [sem((2,))] * 4
        + [sem((16,))] * 2
        + [sem((1,))] * 2
        + [sem((15,))] * 2
        + [sem((3,))] * 2
        + [sem((15,))] * 2
        + [sem((16,))] * 2
        + [sem((2,)), sem((16,))],
        compiler_params=pltpu.CompilerParams(collective_id=1, has_side_effects=True, vmem_limit_bytes=58 << 20),
        name="gather_gram",
    )(ht_all, delta)


def local_energy(spins, offdiag):
    side_sites = math.isqrt(spins.shape[1])
    spin_signs = (2 * spins - 1).astype(jnp.float32).reshape(spins.shape[0], side_sites, side_sites)
    right_spin = jnp.roll(spin_signs, -1, axis=2)
    down_spin = jnp.roll(spin_signs, -1, axis=1)
    diag_one = jnp.roll(down_spin, -1, axis=2)
    diag_two = jnp.roll(down_spin, 1, axis=2)
    near_bonds = jnp.sum(spin_signs * right_spin + spin_signs * down_spin, axis=(1, 2))
    far_bonds = jnp.sum(spin_signs * diag_one + spin_signs * diag_two, axis=(1, 2))
    return 0.25 * (near_bonds + SECOND_RATIO * far_bonds) + offdiag


def per_device(stream, weight_in, weight_out, readout, spins, offdiag):
    samples = spins.shape[0]
    norm_scale = 1.0 / math.sqrt(samples)
    ht_all, delta = forward(jnp.transpose(stream, (1, 0, 2)), weight_in, weight_out, readout[None, :])
    centered, gram = gather_gram(ht_all, delta)
    energies = local_energy(spins, offdiag)
    target = (energies - jnp.mean(energies)) * norm_scale
    return solve(gram, target[None, :], centered)


def solution(mesh):
    return jax.shard_map(
        per_device,
        mesh=mesh,
        in_specs=(P("samp", None, None), P("samp", "par"), P("par", None), P(), P(), P()),
        out_specs=P("samp", "par"),
        check_vma=False,
    )
```

time: 619 us -> 121 us (0.20)
  waiting for transfers between devices: 320 us -> 0 us
  other arithmetic: 170 us -> 1.54 us
  Pallas kernels: 0 us -> 118 us
  matrix products: 46 us -> 0 us
  local copies, waits for them, and re-layouts: 40.7 us -> 0.3 us
  between operations: 18 us -> 0.94 us
  blocking collectives: 14.9 us -> 0 us
    psum x2 -> x0, waiting for transfers between devices: 227 us -> none  [the longest x1 129 us: per_device(): system = lax.psum(shifted, ('samp', 'par'))]
    another operation x18 -> x0, other arithmetic: 118 us -> none  [the longest x14 78.6 us: per_device(): lower_factor = jnp.linalg.cholesky(system)]
    pallas_call x0 -> x3, Pallas kernels: none -> 118 us  [the longest x1 50.2 us: gather_gram(): pl.pallas_call(gather_gram_kernel, out_shape=[jax.ShapeDtypeStruct((512,...]
    all_to_all x1 -> x0, waiting for transfers between devices: 93.1 us -> none  [per_device(): lax.all_to_all(gradients, 'samp', split_axis=1, concat_axis=0, tiled=True)]
    dot_general x6 -> x0, matrix products: 40.4 us -> none  [the longest x1 16.8 us: per_device(): jnp.dot(coeffs[None, :], centered, preferred_element_type=jnp.float32)]
    convert_element_type x3 -> x0, other arithmetic: 28.6 us -> none  [the longest x1 16.8 us: per_device(): ((widened - sample_mean) * norm_scale).astype(jnp.bfloat16)]
    convert_element_type x3 -> x0, local copies, waits for them, and re-layouts: 27.1 us -> none  [the longest x1 14.1 us: per_device(): widened = gradient_panel.astype(jnp.float32)]
    reduce_sum x4 -> x1, other arithmetic: 20 us -> 0.6 us  [per_device(): target = (energies - jnp.mean(energies)) * norm_scale]
  transfers between devices with their start and end apart: 3 -> 0, of which waited for: 3 -> 0; matrix products, arithmetic and copies ran while one was open for 2% -> 0% of each run, Pallas kernels for 0% -> 0%
where the time goes in v1:
time: 121 us; the launch traced here: 120 us
  Pallas kernels  118 us (98%)
  other arithmetic  1.54 us (1%)
    pallas_call x1, Pallas kernels, gather_gram(): pl.pallas_call(gather_gram_kernel, out_shape=[jax.ShapeDtypeStruct((512,...  50.2 us
    pallas_call x1, Pallas kernels, forward(): pl.pallas_call(forward_kernel, out_shape=[jax.ShapeDtypeStruct((8, 16, 64...  46.1 us
    pallas_call x1, Pallas kernels, solve(): pl.pallas_call(functools.partial(solve_kernel, SHIFT_RATIO, -math.sqrt(D...  21.5 us

profile of v1, /device:TPU:1, one launch (start us, length us, event | category | flops | bytes accessed | tf_op | source)
XLA Modules:
  0.0 120.5 jit_solution(17259808676119461851)
XLA Ops:
  0.0 0.0 copy-start
  0.0 46.1 %forward.1 = (bf16[8,16,64,128]{3,2,1,0:T(8,128)(2,1)}, bf16[16,112,128]{2,1,0:T(8,128)(2,1)}) custom-call(f32[25,64,512]{2,1,0:T(8,128)} %bitcast.9, bf16[64,128]{1,0:T(8,128)(2,1)} %win_ref.1, bf16[128,512]{1,0:T(8,128)(2,1)} %wout_ref.1, f32[1,512]{1,0:T(1,128)} %bitcast.11), custom_call_target="tpu_custom_call" | custom-call | tf_op jit(solution)/shard_map/forward/pallas_call | solution.py:373
  46.1 50.2 %gather_gram.1 = (bf16[512,8192]{1,0:T(8,128)(2,1)}, f32[1280,128]{1,0:T(8,128)}) custom-call(bf16[8,16,64,128]{3,2,1,0:T(8,128)(2,1)} %get-tuple-element.9.hall_ref, bf16[16,112,128]{2,1,0:T(8,128)(2,1)} %get-tuple-element.10.dl_ref), custom_call_target="tpu_custom_call" | custom-call | tf_op jit(solution)/shard_map/gather_gram/pallas_call | solution.py:594
  96.3 0.0 copy-done
  96.3 0.0 copy-start.1
  96.4 0.1 fusion.2
  96.5 0.1 maximum_add_fusion
  96.7 0.1 fusion
  96.8 0.1 multiply_reduce_fusion
  96.9 0.1 copy-done.1
  97.0 0.6 fusion.5
  98.3 0.6 subtract_multiply_fusion
  98.9 21.5 %solve.1 = f32[64,128]{1,0:T(8,128)} custom-call(f32[1280,128]{1,0:T(8,128)} %get-tuple-element.11.gram_ref, f32[1,512]{1,0:T(1,128)} %bitcast.10, bf16[512,8192]{1,0:T(8,128)(2,1)} %get-tuple-element.12.cent_hbm), custom_call_target="tpu_custom_call" | custom-call | tf_op jit(solution)/shard_map/solve/pallas_call | solution.py:141
  (9 shorter events, 0.2 us)
Async XLA Ops:
  0.0 96.3 %copy-start = (s32[512,100]{0,1:T(8,128)S(1)}, s32[512,100]{0,1:T(8,128)}, u32[]{:S(2)}) copy-start(s32[512,100]{0,1:T(8,128)} %param.10) | copy-start | bytes 614404
  96.3 0.7 copy-start.1

commit v2 on v1

v2 whole, which is shorter than its diff:
```python
import functools
import math

import jax
import jax.numpy as jnp
from jax import lax
from jax.experimental import pallas as pl
from jax.experimental.pallas import tpu as pltpu
from jax.sharding import PartitionSpec as P

D = 512
FF = 2048
EPSILON = 1e-05
SHIFT_RATIO = 0.1
SECOND_RATIO = 0.5
MESH = pl.DeviceIdType.MESH
F32 = jnp.float32
BF16 = jnp.bfloat16
HI = lax.Precision.HIGHEST


def dot_nn(a, b):
    return lax.dot_general(a, b, (((1,), (0,)), ((), ())), precision=HI, preferred_element_type=F32)


def dot_nt(a, b):
    return lax.dot_general(a, b, (((1,), (1,)), ((), ())), precision=HI, preferred_element_type=F32)


def thirds(values):
    high = values.astype(BF16).astype(F32)
    rest = values - high
    middle = rest.astype(BF16).astype(F32)
    return high, middle, rest - middle


def outer(left, right):
    a, b, c = thirds(left)
    d, e, f = thirds(right)
    lhs = jnp.concatenate([a, a, b, a, b, c], axis=0).astype(BF16)
    rhs = jnp.concatenate([d, e, d, f, e, d], axis=0).astype(BF16)
    return lax.dot_general(lhs, rhs, (((0,), (0,)), ((), ())), preferred_element_type=F32)


def spread_column(values, at):
    return jnp.broadcast_to(values[:, at : at + 1], (8, 128))


def pick(values, row):
    return jnp.broadcast_to(values[row : row + 1, :], (8, 128))


def sweep_block(block):
    lane = lax.broadcasted_iota(jnp.int32, (8, 128), 1)
    sub = lax.broadcasted_iota(jnp.int32, (8, 128), 0)
    units = [jnp.where(sub == i, 1.0, 0.0) for i in range(8)]
    rows = [block[8 * r : 8 * r + 8, :] for r in range(16)]
    splat = [spread_column(rows[0], m) for m in range(8)]
    for g in range(16):
        panel = rows[g]
        before = panel
        last = g == 15
        ahead = [] if last else [spread_column(panel, 8 * g + 8 + m) for m in range(8)]
        old = [] if last else [spread_column(rows[g + 1], 8 * g + 8 + m) for m in range(8)]
        near = {r: [spread_column(rows[r], 8 * g + m) for m in range(8)] for r in (g + 1, g + 2) if r < 16}
        for i in range(8):
            factor = (splat[i] - units[i]) * (1.0 / pick(splat[i], i))
            panel = jnp.where(lane == 8 * g + i, units[i], panel)
            panel = panel - factor * pick(panel, i)
            for m in range(i + 1, 8):
                splat[m] = splat[m] - factor * pick(splat[m], i)
            ahead = [values - factor * pick(values, i) for values in ahead]
        if not last:
            splat = []
            for m in range(8):
                parts = [near[g + 1][j] * pick(ahead[m], j) for j in range(8)]
                even = (parts[0] + parts[2]) + (parts[4] + parts[6])
                odd = (parts[1] + parts[3]) + (parts[5] + parts[7])
                splat.append(old[m] - (even + odd))
        inside = (lane >= 8 * g) & (lane < 8 * g + 8)
        panel = jnp.where(inside, -panel, panel)
        change = outer(before, panel)
        spread = [pick(panel, m) for m in range(8)]
        for r in range(16):
            if r == g:
                continue
            kept = jnp.where(inside, 0.0, rows[r])
            if r in near:
                parts = [near[r][m] * spread[m] for m in range(8)]
                even = (parts[0] + parts[2]) + (parts[4] + parts[6])
                odd = (parts[1] + parts[3]) + (parts[5] + parts[7])
                rows[r] = kept - (even + odd)
            else:
                rows[r] = kept - change[8 * r : 8 * r + 8, :]
        rows[g] = panel
    return jnp.concatenate(rows, axis=0)


def solve_kernel(shift_ratio, scale, samples, gram_ref, target_ref, cent_hbm, out_ref, a_ref, w_ref, cent, sems):
    blocks = samples // 128
    chunks = sems.shape[0]
    wide = cent.shape[1] // chunks

    def load(m):
        at = pl.ds(m * wide, wide)
        return pltpu.make_async_copy(cent_hbm.at[:, at], cent.at[:, at], sems.at[m])

    for m in range(chunks):
        load(m).start()
    eye = lax.broadcasted_iota(jnp.int32, (128, 128), 0) == lax.broadcasted_iota(jnp.int32, (128, 128), 1)
    base = [0]
    for k in range(blocks):
        base.append(base[-1] + samples - 128 * k)
    trace = jnp.zeros((1, 1), F32)
    for k in range(blocks):
        trace += jnp.sum(jnp.where(eye, gram_ref[base[k] : base[k] + 128, :], 0.0), axis=(0, 1), keepdims=True)
    shift = shift_ratio * trace / samples
    shift = jnp.where(eye, jnp.broadcast_to(shift, (128, 128)), 0.0)
    rhs = []
    for k in range(blocks):
        a_ref[base[k] : base[k] + 128, :] = gram_ref[base[k] : base[k] + 128, :] + shift
        if k < blocks - 1:
            a_ref[base[k] + 128 : base[k + 1], :] = gram_ref[base[k] + 128 : base[k + 1], :]
        rhs.append(jnp.broadcast_to(target_ref[0:1, 128 * k : 128 * k + 128], (8, 128)))
    for k in range(blocks):
        inv = -sweep_block(a_ref[base[k] : base[k] + 128, :])
        if k < blocks - 1:
            below = a_ref[base[k] + 128 : base[k + 1], :]
            w = dot_nn(below, inv)
            w_ref[base[k] + 128 : base[k + 1], :] = w
            drop = dot_nt(rhs[k], w)
            for j in range(k + 1, blocks):
                at = 128 * (j - k - 1)
                a_ref[base[j] : base[j + 1], :] -= dot_nt(w[at:], below[at : at + 128])
                rhs[j] = rhs[j] - drop[:, at : at + 128]
        rhs[k] = dot_nn(rhs[k], inv)
    found = [None] * blocks
    for k in reversed(range(blocks)):
        x = rhs[k]
        for i in range(k + 1, blocks):
            r = base[k] + 128 * (i - k)
            x = x - dot_nn(found[i], w_ref[r : r + 128, :])
        found[k] = x
    coeffs = jnp.concatenate(found, axis=1).astype(BF16)
    for m in range(chunks):
        load(m).wait()
        part = jnp.dot(coeffs, cent[:, m * wide : (m + 1) * wide], preferred_element_type=F32) * scale
        for i in range(wide // 128):
            r = m * wide // 128 + i
            out_ref[r : r + 1, :] = part[0:1, 128 * i : 128 * (i + 1)]


def solve(gram, target, centered):
    samples, width = centered.shape
    blocks = samples // 128
    rows = blocks * (blocks + 1) // 2 * 128
    vmem = pl.BlockSpec(memory_space=pltpu.VMEM)
    return pl.pallas_call(
        functools.partial(solve_kernel, SHIFT_RATIO, -math.sqrt(D * FF), samples),
        out_shape=jax.ShapeDtypeStruct((width // 128, 128), F32),
        in_specs=[vmem, vmem, pl.BlockSpec(memory_space=pl.ANY)],
        out_specs=vmem,
        scratch_shapes=[
            pltpu.VMEM((rows, 128), F32),
            pltpu.VMEM((rows, 128), F32),
            pltpu.VMEM((samples, width), BF16),
            pltpu.SemaphoreType.DMA((8,)),
        ],
        compiler_params=pltpu.CompilerParams(vmem_limit_bytes=60 << 20),
        name="solve",
    )(gram, target, centered)


LSIDE = 10
GROUP = 4
WIDE = 8 * 65


def enter(ids):
    barrier = pltpu.get_barrier_semaphore()
    for device in ids:
        pl.semaphore_signal(barrier, inc=1, device_id=device, device_id_type=MESH)
    pl.semaphore_wait(barrier, len(ids))


def remote(src, dst, send, recv, device):
    copy = pltpu.make_async_remote_copy(
        src_ref=src, dst_ref=dst, send_sem=send, recv_sem=recv, device_id=device, device_id_type=MESH
    )
    copy.start()
    return copy


def describe(src, dst, send, recv, device):
    return pltpu.make_async_remote_copy(
        src_ref=src, dst_ref=dst, send_sem=send, recv_sem=recv, device_id=device, device_id_type=MESH
    )


def each(first, last, body):
    def step(k, carry):
        body(k)
        return carry

    lax.fori_loop(first, last, step, 0)


def make_target(spins_ref, offdiag_ref, norm_scale):
    signs = (2 * spins_ref[...] - 1).astype(F32)
    sites = signs.shape[0]
    column = lax.rem(lax.broadcasted_iota(jnp.int32, signs.shape, 0), LSIDE)

    def turn(values, by):
        return jnp.concatenate([values[by:], values[:by]], axis=0)

    def next_column(values):
        return jnp.where(column == LSIDE - 1, turn(values, sites - LSIDE + 1), turn(values, 1))

    def last_column(values):
        return jnp.where(column == 0, turn(values, LSIDE - 1), turn(values, sites - 1))

    down = turn(signs, LSIDE)
    near = jnp.sum(signs * (next_column(signs) + down), axis=0, keepdims=True)
    distant = jnp.sum(signs * (next_column(down) + last_column(down)), axis=0, keepdims=True)
    energies = 0.25 * (near + SECOND_RATIO * distant) + offdiag_ref[...]
    return (energies - jnp.mean(energies, axis=1, keepdims=True)) * norm_scale


def main_kernel(
    stream_ref, win_ref, wout_ref, readout_ref, spins_ref, offdiag_ref, cent_out, gram_ref, target_ref,
    win, wout, hid, ht, hall, slope, acc, dsend, dl, dall, grad, cent, part_ref, twin, first, second,
    xs, xr, ws, wr, vs, vr, wws, wwr, vvs, vvr, sws, swr, svs, svr, hs, hr, ls, lr,
    sr, rr, sl, rl, fr, qr, fl, ql, bs, br, s0, r0, s1, r1, s2, r2, s3, r3, s4, r4, own, outs,
):
    s, p = lax.axis_index("samp"), lax.axis_index("par")
    x, c = s // 2, lax.rem(s, 2)
    y, z = p // 4, lax.rem(p, 4)
    sibling = s + 1 - 2 * c
    n = 16
    groups, tokens = 16, 25
    rows, dims, width, samples = 112, 64, 128, 512
    norm_scale = 1.0 / math.sqrt(samples)
    right, left, far = lax.rem(s + 2, 8), lax.rem(s + 6, 8), lax.rem(s + 4, 8)
    pars = [lax.rem(p + k, 16) for k in range(1, 16)]
    enter([(s, lax.rem(p + k, n)) for k in range(1, n)] + [(lax.rem(s + k, 8), p) for k in range(1, 8)])

    def at(a, b):
        return lax.rem(y + a, 4) * 4 + lax.rem(z + b, 4)

    def origin(a, b):
        return at(4 - a, 4 - b)

    def xcopy(k):
        return describe(win_ref, win.at[p, x, c], xs.at[k - 1], xr.at[k - 1], (lax.rem(s + 2 * k, 8), p))

    def w_first(k):
        return describe(win.at[p, :, c], win.at[p, :, c], ws.at[k - 1], wr.at[k - 1], (s, at(k, 0)))

    def w_then(a, m):
        q, i = origin(a, 0), 3 * a + m - 1
        return describe(win.at[q, :, c], win.at[q, :, c], wws.at[i], wwr.at[i], (s, at(0, m)))

    def v_first(k):
        return describe(wout.at[p, c], wout.at[p, c], vs.at[k - 1], vr.at[k - 1], (s, at(0, k)))

    def v_then(b, m):
        q, i = origin(0, b), 3 * b + m - 1
        return describe(wout.at[q, c], wout.at[q, c], vvs.at[i], vvr.at[i], (s, at(m, 0)))

    def w_across(i):
        q = origin(i // 4, lax.rem(i, 4))
        return describe(win.at[q, :, c], win.at[q, :, c], sws.at[i], swr.at[i], (sibling, p))

    def v_across(i):
        q = origin(i // 4, lax.rem(i, 4))
        return describe(wout.at[q, c], wout.at[q, c], svs.at[i], svr.at[i], (sibling, p))

    def hcopy(k, c):
        to, at_c, i = lax.rem(s + k, 8), pl.ds(pl.multiple_of(4 * c, 4), 4), 4 * (k - 1) + c
        return describe(ht.at[to, at_c], hall.at[s, at_c], hs.at[i], hr.at[i], (to, p))

    def lcopy(k):
        q = lax.rem(p + k, n)
        return describe(dsend.at[q], dl.at[p], ls.at[k - 1], lr.at[k - 1], (s, q))

    mine_w = pltpu.make_async_copy(win_ref, win.at[p, x, c], own.at[0])
    mine_v = pltpu.make_async_copy(wout_ref.at[pl.ds(pl.multiple_of(64 * c, 64), 64)], wout.at[p, c], own.at[1])
    mine_w.start()
    mine_v.start()
    each(1, 4, lambda k: xcopy(k).start())
    mine_v.wait()
    each(1, 4, lambda k: v_first(k).start())
    each(1, 4, lambda m: v_then(0, m).start())
    v_across(0).start()
    mine_w.wait()

    def prepare(four):
        for v in range(2):
            pair = 2 * four + v
            values = stream_ref[:, pl.ds(pl.multiple_of(8 * pair, 8), 8), :]
            mean = jnp.mean(values, axis=-1, keepdims=True)
            centered = values - mean
            variance = jnp.mean(centered * centered, axis=-1, keepdims=True)
            scaled = centered * lax.rsqrt(variance + EPSILON)
            for half in range(2):
                u = 2 * v + half
                g = 4 * four + u
                pieces = [jnp.zeros((4 * u, 512), F32)] if u > 0 else []
                pieces += [scaled[t, 4 * half : 4 * half + 4] for t in range(tokens)]
                pieces += [jnp.zeros((width - 4 * tokens - 4 * u, 512), F32)]
                hidden = jnp.concatenate(pieces, axis=0)

                @pl.when(g == p)
                def _(hidden=hidden):
                    hid[...] = hidden[:rows].astype(BF16)

                flipped = jnp.transpose(hidden).astype(BF16)
                for q in range(8):
                    ht[q, g] = flipped[64 * q : 64 * (q + 1), :]

    def open_w():
        each(1, 4, lambda k: xcopy(k).wait_recv())
        each(1, 4, lambda k: w_first(k).start())
        each(1, 4, lambda m: w_then(0, m).start())
        w_across(0).start()

    def pass_v(k):
        v_first(k).wait_recv()
        each(1, 4, lambda m: v_then(k, m).start())
        v_across(k).start()

    def pass_w(k):
        w_first(k).wait_recv()
        each(1, 4, lambda m: w_then(k, m).start())
        w_across(4 * k).start()

    def work(step):
        @pl.when(step == 1)
        def _():
            each(1, 4, pass_v)

        @pl.when(step == 2)
        def _():
            each(1, 4, pass_w)

        prepare(step)
        each(1, 8, lambda k: hcopy(k, step).start())

        @pl.when(step == 0)
        def _():
            open_w()

    each(0, 4, work)
    mine_h = pltpu.make_async_copy(ht.at[s], hall.at[s], own.at[2])
    mine_h.start()
    target_ref[...] = make_target(spins_ref, offdiag_ref, norm_scale)
    acc[...] = jnp.zeros_like(acc)

    def take(a):
        for b in range(4):
            if b > 0:
                w_then(a, b).wait_recv()
                w_across(4 * a + b).start()

            @pl.when(a > 0)
            def _():
                v_then(b, a).wait_recv()
                v_across(4 * a + b).start()

    def compute(a):
        row = lax.rem(y - a + 4, 4)
        for b in range(4):
            w_across(4 * a + b).wait_recv()
            v_across(4 * a + b).wait_recv()
        weights = jnp.concatenate([win[4 * row + j].reshape(512, 128) for j in range(4)], axis=1)
        preact = jnp.dot(hid[...], weights, preferred_element_type=F32)
        active, pull = jax.vjp(jax.nn.gelu, preact)
        slope[row] = pull(jnp.ones_like(preact))[0]
        acc[...] += jnp.dot(active.astype(BF16), wout[pl.ds(4 * row, 4)].reshape(512, 512), preferred_element_type=F32)

    take(0)

    def both(a):
        take(a)
        compute(a - 1)

    each(1, 4, both)
    compute(3)
    signal = (readout_ref[...] * jnp.tanh(acc[...])).astype(BF16)

    def back(i):
        row = lax.rem(y + jnp.where(i < 2, i, 5 - i), 4)
        weights = wout[pl.ds(4 * row, 4)].reshape(512, 512)
        backward = lax.dot_general(signal, weights, (((1,), (1,)), ((), ())), preferred_element_type=F32)
        delta = (backward * slope[row]).astype(BF16)
        for j in range(4):
            q = 4 * row + j
            dsend[q] = delta[:, 128 * j : 128 * (j + 1)]

            @pl.when(q != p)
            def _():
                lcopy(lax.rem(q - p + n, n)).start()

    each(0, 4, back)
    dl[p] = dsend[p]

    def chunk(i):
        return lax.rem(y + jnp.where(i == 0, 0, jnp.where(i == 1, 3, i - 1)), 4)

    def move(origin, i, send, recv, device):
        part = dall.at[origin, chunk(i)]
        return describe(part, part, send, recv, device)

    def to_right(i):
        return move(s, i, sr.at[i], rr.at[i], (right, p))

    def to_left(i):
        return move(s, i, sl.at[i], rl.at[i], (left, p))

    def on_right(j):
        return move(left, 2 * j, fr.at[j], qr.at[j], (right, p))

    def on_left(j):
        return move(right, 2 * j + 1, fl.at[j], ql.at[j], (left, p))

    def across(origin, i, slot):
        return move(origin, i, bs.at[slot + i], br.at[slot + i], (sibling, p))

    def begin(i):
        f = chunk(i)
        for j in range(4):
            q = 4 * f + j

            @pl.when(q != p)
            def _(q=q):
                lcopy(lax.rem(p - q + n, n)).wait_recv()

        for u in range(4):
            window = dl[4 * f + u]
            dall[s, f, 96 * u + 16 : 96 * u + 96, :] = window[16:96]
            if u == 0:
                dall[s, f, 0:16, :] = window[0:16]
            else:
                dall[s, f, 96 * u : 96 * u + 16, :] = window[0:16] + dl[4 * f + u - 1][96:112]
            if u == 3:
                dall[s, f, 384:400, :] = window[96:112]
        to_right(i).start()
        to_left(i).start()
        across(s, i, 0).start()

    each(0, 4, begin)
    mine_h.wait()

    lane = lax.broadcasted_iota(jnp.int32, (dims, width), 1)
    keep = [lax.rem(lane, GROUP) == i for i in range(GROUP)]
    fill = jnp.zeros((width - rows, 128), BF16)
    nothing = jnp.zeros((dims, width), BF16)

    def make(origin, i):
        f = chunk(i)
        for u in range(4):
            group = 4 * f + u
            flipped = hall[origin, group]
            delta = jnp.concatenate([dall[origin, f, 96 * u : 96 * u + rows, :], fill], axis=0)
            stack = jnp.concatenate([jnp.where(keep[v], flipped, nothing) for v in range(GROUP)], axis=0)
            grads = jnp.dot(stack, delta, preferred_element_type=F32).astype(BF16).astype(F32)
            for v in range(GROUP):
                grad[pl.ds(64 * origin + GROUP * group + v, dims, stride=WIDE), :] = grads[dims * v : dims * (v + 1), :]

    each(0, 4, lambda i: make(s, i))
    each(1, 8, lambda k: each(0, 4, lambda f: hcopy(k, f).wait_recv()))

    def near(i):
        to_right(i).wait_recv()
        to_left(i).wait_recv()

        @pl.when(lax.rem(i, 2) == 0)
        def _():
            on_right(i // 2).start()

        @pl.when(lax.rem(i, 2) == 1)
        def _():
            on_left(i // 2).start()

        across(left, i, 4).start()
        across(right, i, 8).start()
        make(left, i)
        make(right, i)

    each(0, 4, near)

    def beside(i):
        across(s, i, 0).wait_recv()
        make(sibling, i)

    each(0, 4, beside)

    def opposite(j):
        on_right(j).wait_recv()
        across(far, 2 * j, 12).start()
        on_left(j).wait_recv()
        across(far, 2 * j + 1, 12).start()
        make(far, 2 * j)
        make(far, 2 * j + 1)

    each(0, 2, opposite)

    def near_beside(i):
        across(left, i, 4).wait_recv()
        across(right, i, 8).wait_recv()
        make(sibling + left - s, i)
        make(sibling + right - s, i)

    each(0, 4, near_beside)

    def far_beside(i):
        across(far, i, 12).wait_recv()
        make(sibling + far - s, i)

    each(0, 4, far_beside)

    count = 4

    def center(m):
        for half in range(count):
            d = count * m + half
            values = grad[d * WIDE : d * WIDE + samples, :]
            mean = jnp.sum(values, axis=0, keepdims=True) * (1.0 / samples)
            cent[:, d * 128 : (d + 1) * 128] = ((values - mean) * norm_scale).astype(BF16)

    def store(m):
        at = pl.ds(m * 128 * count, 128 * count)
        return pltpu.make_async_copy(cent.at[:, at], cent_out.at[:, at], outs.at[m])

    def add(m):
        block = cent[:, m * 128 * count : (m + 1) * 128 * count]
        low = lax.dot_general(block, block[:256], (((1,), (1,)), ((), ())), preferred_element_type=F32)
        high = lax.dot_general(block[256:], block[256:], (((1,), (1,)), ((), ())), preferred_element_type=F32)
        for a, b, term in [(0, 512, low[:, :128]), (512, 896, low[128:, 128:]), (896, 1152, high[:, :128]), (1152, 1280, high[128:, 128:])]:
            if m == 0:
                part_ref[a:b, :] = term
            else:
                part_ref[a:b, :] += term

    steps = dims // count
    center(0)
    store(0).start()
    for m in range(1, steps):
        center(m)
        store(m).start()
        add(m - 1)
    add(steps - 1)

    core = c

    def slot(half, q):
        return pl.ds(pl.multiple_of(640 * half + 40 * q, 8), 40)

    give = pl.ds(pl.multiple_of(640 * (1 - core), 640), 640)
    keeps = pl.ds(pl.multiple_of(640 * core, 640), 640)
    copy = remote(part_ref.at[give], twin, s0.at[0], r0.at[0], (sibling, p))
    copy.wait_recv()
    part_ref[keeps, :] += twin[...]
    copies = [remote(part_ref.at[slot(core, q)], first.at[p], s1.at[k], r1.at[k], (s, q)) for k, q in enumerate(pars)]
    first[p] = part_ref[slot(core, p), :]
    for each_copy in copies:
        each_copy.wait_recv()
    total = first[0]
    for q in range(1, 16):
        total = total + first[q]
    second[x] = total
    more = [remote(second.at[x], second.at[x], s2.at[k], r2.at[k], (q, p)) for k, q in enumerate([right, far, left])]
    for each_copy in more:
        each_copy.wait_recv()
    total = second[0]
    for q in range(1, 4):
        total = total + second[q]
    gram_ref[slot(core, p), :] = total
    here = gram_ref.at[slot(core, p)]
    spread = [remote(here, here, s3.at[k], r3.at[k], (s, q)) for k, q in enumerate(pars)]
    passed = [remote(here, here, s4.at[15], r4.at[15], (sibling, p))]
    for k in range(15):
        spread[k].wait_recv()
        there = gram_ref.at[slot(core, lax.rem(p + 15 - k, 16))]
        passed.append(remote(there, there, s4.at[k], r4.at[k], (sibling, p)))
    for each_copy in passed:
        each_copy.wait()
    copy.wait_send()
    for each_copy in copies + more + spread:
        each_copy.wait_send()
    each(0, 4, lambda c: to_right(c).wait_send())
    each(0, 4, lambda c: to_left(c).wait_send())
    each(0, 2, lambda c: on_right(c).wait_send())
    each(0, 2, lambda c: on_left(c).wait_send())
    each(0, 4, lambda i: each(0, 4, lambda j: across(s, i, 4 * j).wait_send()))
    for m in range(steps):
        store(m).wait()
    each(1, n, lambda k: lcopy(k).wait_send())
    each(1, 8, lambda k: each(0, 4, lambda c: hcopy(k, c).wait_send()))
    each(1, 4, lambda k: xcopy(k).wait_send())
    each(1, 4, lambda k: w_first(k).wait_send())
    each(1, 4, lambda k: v_first(k).wait_send())
    each(0, 4, lambda k: each(1, 4, lambda m: w_then(k, m).wait_send()))
    each(0, 4, lambda k: each(1, 4, lambda m: v_then(k, m).wait_send()))
    each(0, n, lambda i: w_across(i).wait_send())
    each(0, n, lambda i: v_across(i).wait_send())


def make_gram(stream, weight_in, weight_out, readout, spins, offdiag):
    rows = 112
    sem = pltpu.SemaphoreType.DMA
    vmem = pl.BlockSpec(memory_space=pltpu.VMEM)
    counts = [3, 3, 3, 12, 12, 16, 16, 28, 15, 4, 4, 2, 2, 16, 1, 15, 3, 15, 16]
    return pl.pallas_call(
        main_kernel,
        out_shape=[
            jax.ShapeDtypeStruct((512, 8192), BF16),
            jax.ShapeDtypeStruct((1280, 128), F32),
            jax.ShapeDtypeStruct((1, 512), F32),
        ],
        in_specs=[vmem] * 6,
        out_specs=[pl.BlockSpec(memory_space=pl.ANY), vmem, vmem],
        scratch_shapes=[
            pltpu.VMEM((16, 4, 2, 64, 128), BF16),
            pltpu.VMEM((16, 2, 64, 512), BF16),
            pltpu.VMEM((rows, 512), BF16),
            pltpu.VMEM((8, 16, 64, 128), BF16),
            pltpu.VMEM((8, 16, 64, 128), BF16),
            pltpu.VMEM((4, rows, 512), F32),
            pltpu.VMEM((rows, 512), F32),
            pltpu.VMEM((16, rows, 128), BF16),
            pltpu.VMEM((16, rows, 128), BF16),
            pltpu.VMEM((8, 4, 400, 128), BF16),
            pltpu.VMEM((64 * WIDE, 128), F32),
            pltpu.VMEM((512, 8192), BF16),
            pltpu.VMEM((1280, 128), F32),
            pltpu.VMEM((640, 128), F32),
            pltpu.VMEM((16, 40, 128), F32),
            pltpu.VMEM((4, 40, 128), F32),
        ]
        + [sem((count,)) for count in counts for _ in range(2)]
        + [sem((3,)), sem((16,))],
        compiler_params=pltpu.CompilerParams(collective_id=1, has_side_effects=True, vmem_limit_bytes=60 << 20),
        name="make_gram",
    )(stream, weight_in, weight_out, readout, spins, offdiag)


def per_device(stream, weight_in, weight_out, readout, spins, offdiag):
    centered, gram, target = make_gram(
        jnp.transpose(stream, (1, 0, 2)), weight_in, weight_out, readout[None, :], jnp.transpose(spins), offdiag[None, :]
    )
    return solve(gram, target, centered)


def solution(mesh):
    return jax.shard_map(
        per_device,
        mesh=mesh,
        in_specs=(P("samp", None, None), P("samp", "par"), P("par", None), P(), P(), P()),
        out_specs=P("samp", "par"),
        check_vma=False,
    )
```

time: 121 us -> 106 us (0.88)
  Pallas kernels: 118 us -> 106 us
  other arithmetic: 1.54 us -> 0 us
    pallas_call x2 -> x1, Pallas kernels: 96.2 us -> 86.5 us  [make_gram(): pl.pallas_call(main_kernel, out_shape=[jax.ShapeDtypeStruct((512, 8192),...]
    pallas_call x1, Pallas kernels: 21.5 us -> 19.4 us  [solve(): pl.pallas_call(functools.partial(solve_kernel, SHIFT_RATIO, -math.sqrt(D...]
where the time goes in v2:
time: 106 us
  Pallas kernels  106 us (100%)
    pallas_call x1, Pallas kernels, make_gram(): pl.pallas_call(main_kernel, out_shape=[jax.ShapeDtypeStruct((512, 8192),...  86.5 us
    pallas_call x1, Pallas kernels, solve(): pl.pallas_call(functools.partial(solve_kernel, SHIFT_RATIO, -math.sqrt(D...  19.4 us

profile of v2, /device:TPU:1, one launch (start us, length us, event | category | flops | bytes accessed | tf_op | source)
XLA Modules:
  0.0 106.0 jit_solution(7885262472073772910)
XLA Ops:
  0.0 86.5 %make_gram.1 = (bf16[512,8192]{1,0:T(8,128)(2,1)}, f32[1280,128]{1,0:T(8,128)}, f32[1,512]{1,0:T(1,128)}) custom-call(f32[25,64,512]{2,1,0:T(8,128)} %bitcast.4, bf16[64,128]{1,0:T(8,128)(2,1)} %win_ref.1, bf16[128,512]{1,0:T(8,128)(2,1)} %wout_ref.1, f32[1,512]{1,0:T(1,128)} %bitcast.6, s32[100,512]{1,0:T(8,128)} %bitcast.5, f32[1,512]{1,0:T(1,128)} %bitcast.7), custom_call_target="tpu_custom_call" | custom-call | tf_op jit(solution)/shard_map/make_gram/pallas_call | solution.py:614
  86.5 19.4 %solve.1 = f32[64,128]{1,0:T(8,128)} custom-call(f32[1280,128]{1,0:T(8,128)} %get-tuple-element.8.gram_ref, f32[1,512]{1,0:T(1,128)} %get-tuple-element.9.target_ref, bf16[512,8192]{1,0:T(8,128)(2,1)} %get-tuple-element.10.cent_hbm), custom_call_target="tpu_custom_call" | custom-call | tf_op jit(solution)/shard_map/solve/pallas_call | solution.py:158

commit v3 on v2

--- a/solution.py
+++ b/solution.py
@@ -50,18 +50,19 @@
     return jnp.broadcast_to(values[row : row + 1, :], (8, 128))
 
 
-def sweep_block(block):
+def sweep_block(block, later):
     lane = lax.broadcasted_iota(jnp.int32, (8, 128), 1)
     sub = lax.broadcasted_iota(jnp.int32, (8, 128), 0)
     units = [jnp.where(sub == i, 1.0, 0.0) for i in range(8)]
     rows = [block[8 * r : 8 * r + 8, :] for r in range(16)]
     splat = [spread_column(rows[0], m) for m in range(8)]
+    ahead = [spread_column(rows[0], 8 + m) for m in range(8)]
     for g in range(16):
         panel = rows[g]
         before = panel
         last = g == 15
-        ahead = [] if last else [spread_column(panel, 8 * g + 8 + m) for m in range(8)]
-        old = [] if last else [spread_column(rows[g + 1], 8 * g + 8 + m) for m in range(8)]
+        beyond = [spread_column(panel, 8 * g + 16 + m) for m in range(8)] if g < 14 else []
+        old = [] if last else [spread_column(rows[g + 1], 8 * g + 8 + m) for m in range(16 if g < 14 else 8)]
         near = {r: [spread_column(rows[r], 8 * g + m) for m in range(8)] for r in (g + 1, g + 2) if r < 16}
         for i in range(8):
             factor = (splat[i] - units[i]) * (1.0 / pick(splat[i], i))
@@ -70,13 +71,15 @@
             for m in range(i + 1, 8):
                 splat[m] = splat[m] - factor * pick(splat[m], i)
             ahead = [values - factor * pick(values, i) for values in ahead]
+            beyond = [values - factor * pick(values, i) for values in beyond]
         if not last:
-            splat = []
-            for m in range(8):
-                parts = [near[g + 1][j] * pick(ahead[m], j) for j in range(8)]
+            fresh = []
+            for m, values in enumerate(ahead + beyond):
+                parts = [near[g + 1][j] * pick(values, j) for j in range(8)]
                 even = (parts[0] + parts[2]) + (parts[4] + parts[6])
                 odd = (parts[1] + parts[3]) + (parts[5] + parts[7])
-                splat.append(old[m] - (even + odd))
+                fresh.append(old[m] - (even + odd))
+            splat, ahead = fresh[:8], fresh[8:]
         inside = (lane >= 8 * g) & (lane < 8 * g + 8)
         panel = jnp.where(inside, -panel, panel)
         change = outer(before, panel)
@@ -93,10 +96,14 @@
             else:
                 rows[r] = kept - change[8 * r : 8 * r + 8, :]
         rows[g] = panel
+        if later:
+            later.pop(0)()
+    while later:
+        later.pop(0)()
     return jnp.concatenate(rows, axis=0)
 
 
-def solve_kernel(shift_ratio, scale, samples, gram_ref, target_ref, cent_hbm, out_ref, a_ref, w_ref, cent, sems):
+def solve_kernel(shift_ratio, scale, samples, gram_ref, target_ref, cent_hbm, out_ref, cent, sems):
     blocks = samples // 128
     chunks = sems.shape[0]
     wide = cent.shape[1] // chunks
@@ -117,29 +124,57 @@
     shift = shift_ratio * trace / samples
     shift = jnp.where(eye, jnp.broadcast_to(shift, (128, 128)), 0.0)
     rhs = []
+    tiles, quot = {}, {}
     for k in range(blocks):
-        a_ref[base[k] : base[k] + 128, :] = gram_ref[base[k] : base[k] + 128, :] + shift
+        for i in range(k, blocks):
+            at = base[k] + 128 * (i - k)
+            tiles[i, k] = gram_ref[at : at + 128, :] + shift if i == k else gram_ref[at : at + 128, :]
+        rhs.append(jnp.broadcast_to(target_ref[0:1, 128 * k : 128 * k + 128], (8, 128)))
+
+    def divide(i, k, inv):
+        def run():
+            quot[i, k] = dot_nn(tiles[i, k], inv)
+
+        return run
+
+    def reduce(i, j, k):
+        def run():
+            tiles[i, j] = tiles[i, j] - dot_nt(quot[i, k], tiles[j, k])
+
+        return run
+
+    def lower(i, k, right):
+        def run():
+            rhs[i] = rhs[i] - dot_nt(right, quot[i, k])
+
+        return run
+
+    def close(k, right, inv):
+        def run():
+            rhs[k] = dot_nn(right, inv)
+
+        return run
+
+    later = []
+    for k in range(blocks):
+        inv = -sweep_block(tiles[k, k], later)
+        later = []
         if k < blocks - 1:
-            a_ref[base[k] + 128 : base[k + 1], :] = gram_ref[base[k] + 128 : base[k + 1], :]
-        rhs.append(jnp.broadcast_to(target_ref[0:1, 128 * k : 128 * k + 128], (8, 128)))
-    for k in range(blocks):
-        inv = -sweep_block(a_ref[base[k] : base[k] + 128, :])
+            divide(k + 1, k, inv)()
+            reduce(k + 1, k + 1, k)()
+            later += [divide(i, k, inv) for i in range(k + 2, blocks)]
+            later += [reduce(i, k + 1, k) for i in range(k + 2, blocks)]
+            later += [reduce(i, j, k) for j in range(k + 2, blocks) for i in range(j, blocks)]
+            later += [lower(i, k, rhs[k]) for i in range(k + 1, blocks)]
         if k < blocks - 1:
-            below = a_ref[base[k] + 128 : base[k + 1], :]
-            w = dot_nn(below, inv)
-            w_ref[base[k] + 128 : base[k + 1], :] = w
-            drop = dot_nt(rhs[k], w)
-            for j in range(k + 1, blocks):
-                at = 128 * (j - k - 1)
-                a_ref[base[j] : base[j + 1], :] -= dot_nt(w[at:], below[at : at + 128])
-                rhs[j] = rhs[j] - drop[:, at : at + 128]
-        rhs[k] = dot_nn(rhs[k], inv)
+            later.append(close(k, rhs[k], inv))
+        else:
+            close(k, rhs[k], inv)()
     found = [None] * blocks
     for k in reversed(range(blocks)):
         x = rhs[k]
         for i in range(k + 1, blocks):
-            r = base[k] + 128 * (i - k)
-            x = x - dot_nn(found[i], w_ref[r : r + 128, :])
+            x = x - dot_nn(found[i], quot[i, k])
         found[k] = x
     coeffs = jnp.concatenate(found, axis=1).astype(BF16)
     for m in range(chunks):
@@ -153,7 +188,6 @@
 def solve(gram, target, centered):
     samples, width = centered.shape
     blocks = samples // 128
-    rows = blocks * (blocks + 1) // 2 * 128
     vmem = pl.BlockSpec(memory_space=pltpu.VMEM)
     return pl.pallas_call(
         functools.partial(solve_kernel, SHIFT_RATIO, -math.sqrt(D * FF), samples),
@@ -161,8 +195,6 @@
         in_specs=[vmem, vmem, pl.BlockSpec(memory_space=pl.ANY)],
         out_specs=vmem,
         scratch_shapes=[
-            pltpu.VMEM((rows, 128), F32),
-            pltpu.VMEM((rows, 128), F32),
             pltpu.VMEM((samples, width), BF16),
             pltpu.SemaphoreType.DMA((8,)),
         ],

time: 106 us -> 106 us (level)
  no operation moved by 1% of the time
where the time goes in v3:
time: 106 us; the launch traced here: 105 us
  Pallas kernels  105 us (99%)
    pallas_call x1, Pallas kernels, make_gram(): pl.pallas_call(main_kernel, out_shape=[jax.ShapeDtypeStruct((512, 8192),...  86.5 us
    pallas_call x1, Pallas kernels, solve(): pl.pallas_call(functools.partial(solve_kernel, SHIFT_RATIO, -math.sqrt(D...  18.8 us

profile of v3, /device:TPU:1, one launch (start us, length us, event | category | flops | bytes accessed | tf_op | source)
XLA Modules:
  0.0 105.4 jit_solution(10154426126432639502)
XLA Ops:
  0.0 86.5 %make_gram.1 = (bf16[512,8192]{1,0:T(8,128)(2,1)}, f32[1280,128]{1,0:T(8,128)}, f32[1,512]{1,0:T(1,128)}) custom-call(f32[25,64,512]{2,1,0:T(8,128)} %bitcast.4, bf16[64,128]{1,0:T(8,128)(2,1)} %win_ref.1, bf16[128,512]{1,0:T(8,128)(2,1)} %wout_ref.1, f32[1,512]{1,0:T(1,128)} %bitcast.6, s32[100,512]{1,0:T(8,128)} %bitcast.5, f32[1,512]{1,0:T(1,128)} %bitcast.7), custom_call_target="tpu_custom_call" | custom-call | tf_op jit(solution)/shard_map/make_gram/pallas_call | solution.py:646
  86.5 18.8 %solve.1 = f32[64,128]{1,0:T(8,128)} custom-call(f32[1280,128]{1,0:T(8,128)} %get-tuple-element.8.gram_ref, f32[1,512]{1,0:T(1,128)} %get-tuple-element.9.target_ref, bf16[512,8192]{1,0:T(8,128)(2,1)} %get-tuple-element.10.cent_hbm), custom_call_target="tpu_custom_call" | custom-call | tf_op jit(solution)/shard_map/solve/pallas_call | solution.py:192

commit v4 on v3

--- a/solution.py
+++ b/solution.py
@@ -663,7 +663,7 @@
             pltpu.VMEM((16, rows, 128), BF16),
             pltpu.VMEM((16, rows, 128), BF16),
             pltpu.VMEM((8, 4, 400, 128), BF16),
-            pltpu.VMEM((64 * WIDE, 128), F32),
+            pltpu.VMEM((65 * WIDE, 128), F32),
             pltpu.VMEM((512, 8192), BF16),
             pltpu.VMEM((1280, 128), F32),
             pltpu.VMEM((640, 128), F32),

time: 106 us -> 105 us (level)
  no operation moved by 1% of the time
where the time goes in v4:
time: 105 us
  Pallas kernels  105 us (100%)
    pallas_call x1, Pallas kernels, make_gram(): pl.pallas_call(main_kernel, out_shape=[jax.ShapeDtypeStruct((512, 8192),...  86.4 us
    pallas_call x1, Pallas kernels, solve(): pl.pallas_call(functools.partial(solve_kernel, SHIFT_RATIO, -math.sqrt(D...  18.8 us

profile of v4, /device:TPU:1, one launch (start us, length us, event | category | flops | bytes accessed | tf_op | source)
XLA Modules:
  0.0 105.4 jit_solution(5720061976427654942)
XLA Ops:
  0.0 86.4 %make_gram.1 = (bf16[512,8192]{1,0:T(8,128)(2,1)}, f32[1280,128]{1,0:T(8,128)}, f32[1,512]{1,0:T(1,128)}) custom-call(f32[25,64,512]{2,1,0:T(8,128)} %bitcast.4, bf16[64,128]{1,0:T(8,128)(2,1)} %win_ref.1, bf16[128,512]{1,0:T(8,128)(2,1)} %wout_ref.1, f32[1,512]{1,0:T(1,128)} %bitcast.6, s32[100,512]{1,0:T(8,128)} %bitcast.5, f32[1,512]{1,0:T(1,128)} %bitcast.7), custom_call_target="tpu_custom_call" | custom-call | tf_op jit(solution)/shard_map/make_gram/pallas_call | solution.py:646
  86.4 18.8 %solve.1 = f32[64,128]{1,0:T(8,128)} custom-call(f32[1280,128]{1,0:T(8,128)} %get-tuple-element.8.gram_ref, f32[1,512]{1,0:T(1,128)} %get-tuple-element.9.target_ref, bf16[512,8192]{1,0:T(8,128)(2,1)} %get-tuple-element.10.cent_hbm), custom_call_target="tpu_custom_call" | custom-call | tf_op jit(solution)/shard_map/solve/pallas_call | solution.py:192

commit v5 on v4

--- a/solution.py
+++ b/solution.py
@@ -259,7 +259,7 @@
 
 
 def main_kernel(
-    stream_ref, win_ref, wout_ref, readout_ref, spins_ref, offdiag_ref, cent_out, gram_ref, target_ref,
+    stream_hbm, win_ref, wout_ref, readout_ref, spins_ref, offdiag_ref, cent_out, gram_ref, target_ref, stream_ref,
     win, wout, hid, ht, hall, slope, acc, dsend, dl, dall, grad, cent, part_ref, twin, first, second,
     xs, xr, ws, wr, vs, vr, wws, wwr, vvs, vvr, sws, swr, svs, svr, hs, hr, ls, lr,
     sr, rr, sl, rl, fr, qr, fl, ql, bs, br, s0, r0, s1, r1, s2, r2, s3, r3, s4, r4, own, outs,
@@ -270,6 +270,8 @@
     sibling = s + 1 - 2 * c
     n = 16
     groups, tokens = 16, 25
+    fetch = pltpu.make_async_copy(stream_hbm, stream_ref, own.at[3])
+    fetch.start()
     rows, dims, width, samples = 112, 64, 128, 512
     norm_scale = 1.0 / math.sqrt(samples)
     right, left, far = lax.rem(s + 2, 8), lax.rem(s + 6, 8), lax.rem(s + 4, 8)
@@ -382,6 +384,7 @@
         def _():
             open_w()
 
+    fetch.wait()
     each(0, 4, work)
     mine_h = pltpu.make_async_copy(ht.at[s], hall.at[s], own.at[2])
     mine_h.start()
@@ -650,9 +653,10 @@
             jax.ShapeDtypeStruct((1280, 128), F32),
             jax.ShapeDtypeStruct((1, 512), F32),
         ],
-        in_specs=[vmem] * 6,
+        in_specs=[pl.BlockSpec(memory_space=pl.ANY)] * 3 + [vmem] * 3,
         out_specs=[pl.BlockSpec(memory_space=pl.ANY), vmem, vmem],
         scratch_shapes=[
+            pltpu.VMEM((25, 64, 512), F32),
             pltpu.VMEM((16, 4, 2, 64, 128), BF16),
             pltpu.VMEM((16, 2, 64, 512), BF16),
             pltpu.VMEM((rows, 512), BF16),
@@ -671,7 +675,7 @@
             pltpu.VMEM((4, 40, 128), F32),
         ]
         + [sem((count,)) for count in counts for _ in range(2)]
-        + [sem((3,)), sem((16,))],
+        + [sem((4,)), sem((16,))],
         compiler_params=pltpu.CompilerParams(collective_id=1, has_side_effects=True, vmem_limit_bytes=60 << 20),
         name="make_gram",
     )(stream, weight_in, weight_out, readout, spins, offdiag)

time: 105 us -> 105 us (level)
  no operation moved by 1% of the time
where the time goes in v5:
time: 105 us
  Pallas kernels  104 us (99%)
    pallas_call x1, Pallas kernels, make_gram(): pl.pallas_call(main_kernel, out_shape=[jax.ShapeDtypeStruct((512, 8192),...  85.7 us
    pallas_call x1, Pallas kernels, solve(): pl.pallas_call(functools.partial(solve_kernel, SHIFT_RATIO, -math.sqrt(D...  18.8 us

profile of v5, /device:TPU:1, one launch (start us, length us, event | category | flops | bytes accessed | tf_op | source)
XLA Modules:
  0.0 104.6 jit_solution(8239059541962141373)
XLA Ops:
  0.0 85.7 %make_gram.1 = (bf16[512,8192]{1,0:T(8,128)(2,1)}, f32[1280,128]{1,0:T(8,128)}, f32[1,512]{1,0:T(1,128)}) custom-call(f32[25,64,512]{2,1,0:T(8,128)} %bitcast.4, bf16[64,128]{1,0:T(8,128)(2,1)} %win_ref.1, bf16[128,512]{1,0:T(8,128)(2,1)} %wout_ref.1, f32[1,512]{1,0:T(1,128)} %bitcast.6, s32[100,512]{1,0:T(8,128)} %bitcast.5, f32[1,512]{1,0:T(1,128)} %bitcast.7), custom_call_target="tpu_custom_call" | custom-call | tf_op jit(solution)/shard_map/make_gram/pallas_call | solution.py:649
  85.7 18.8 %solve.1 = f32[64,128]{1,0:T(8,128)} custom-call(f32[1280,128]{1,0:T(8,128)} %get-tuple-element.8.gram_ref, f32[1,512]{1,0:T(1,128)} %get-tuple-element.9.target_ref, bf16[512,8192]{1,0:T(8,128)(2,1)} %get-tuple-element.10.cent_hbm), custom_call_target="tpu_custom_call" | custom-call | tf_op jit(solution)/shard_map/solve/pallas_call | solution.py:192

commit v6 on v5

--- a/solution.py
+++ b/solution.py
@@ -276,7 +276,8 @@
     norm_scale = 1.0 / math.sqrt(samples)
     right, left, far = lax.rem(s + 2, 8), lax.rem(s + 6, 8), lax.rem(s + 4, 8)
     pars = [lax.rem(p + k, 16) for k in range(1, 16)]
-    enter([(s, lax.rem(p + k, n)) for k in range(1, n)] + [(lax.rem(s + k, 8), p) for k in range(1, 8)])
+    lines = [(s, lax.rem(y + k, 4) * 4 + z) for k in range(1, 4)] + [(s, y * 4 + lax.rem(z + k, 4)) for k in range(1, 4)]
+    enter(lines + [(lax.rem(s + k, 8), p) for k in range(1, 8)])
 
     def at(a, b):
         return lax.rem(y + a, 4) * 4 + lax.rem(z + b, 4)

time: 105 us -> 104 us (level)
  no operation moved by 1% of the time
where the time goes in v6:
time: 104 us
  Pallas kernels  104 us (100%)
    pallas_call x1, Pallas kernels, make_gram(): pl.pallas_call(main_kernel, out_shape=[jax.ShapeDtypeStruct((512, 8192),...  85.3 us
    pallas_call x1, Pallas kernels, solve(): pl.pallas_call(functools.partial(solve_kernel, SHIFT_RATIO, -math.sqrt(D...  18.8 us

profile of v6, /device:TPU:1, one launch (start us, length us, event | category | flops | bytes accessed | tf_op | source)
XLA Modules:
  0.0 104.3 jit_solution(12544942005980241595)
XLA Ops:
  0.0 85.3 %make_gram.1 = (bf16[512,8192]{1,0:T(8,128)(2,1)}, f32[1280,128]{1,0:T(8,128)}, f32[1,512]{1,0:T(1,128)}) custom-call(f32[25,64,512]{2,1,0:T(8,128)} %bitcast.4, bf16[64,128]{1,0:T(8,128)(2,1)} %win_ref.1, bf16[128,512]{1,0:T(8,128)(2,1)} %wout_ref.1, f32[1,512]{1,0:T(1,128)} %bitcast.6, s32[100,512]{1,0:T(8,128)} %bitcast.5, f32[1,512]{1,0:T(1,128)} %bitcast.7), custom_call_target="tpu_custom_call" | custom-call | tf_op jit(solution)/shard_map/make_gram/pallas_call | solution.py:650
  85.3 18.8 %solve.1 = f32[64,128]{1,0:T(8,128)} custom-call(f32[1280,128]{1,0:T(8,128)} %get-tuple-element.8.gram_ref, f32[1,512]{1,0:T(1,128)} %get-tuple-element.9.target_ref, bf16[512,8192]{1,0:T(8,128)(2,1)} %get-tuple-element.10.cent_hbm), custom_call_target="tpu_custom_call" | custom-call | tf_op jit(solution)/shard_map/solve/pallas_call | solution.py:192
